TPU v7x, 128 devices: a whole 4x4x4 slice. The times are simulated.
128 devices in a mesh: group: 8 (over y, core), path: 16 (over z, x).
Axes of the slice: x: 4, y: 4, z: 4, core: 2. Of those that a mesh axis runs over, the one named last changes fastest.
Arguments:
- inner_params: float32 [256, 2, 32768], P(('group', 'path')), may hold values from -6 to 6
- route: int32 [256, 2], replicated, may hold values from 0 to 15, as said below
- owner: int32 [2, 16], replicated, may hold values from 0 to 127, as said below
- outer_state: float32 [128, 32768], P(('group', 'path')), may hold values from -6 to 6
- momentum: float32 [128, 32768], P(('group', 'path')), may hold values from -4 to 4
Outputs:
- snapshots: float32 [256, 2, 32768], P(('group', 'path'))
- new_momentum: float32 [128, 32768], P(('group', 'path'))
Inputs may be any that keep to these rules, and one draw needn't show every extreme that they name: `route`: every module of each level is used by one or more paths. `owner`: the 32 entries are distinct devices.
All inputs are finite; a program needn't handle non-finite values.
Results may differ from a plain program's by a relative error of at most 0.00007.
Values sent between devices are 32-bit elements; how exact they have to be, the bound alone decides.
A program may use at most 128 MiB of HBM per device.

v0:
```python
import jax
import jax.numpy as jnp
from jax import lax
from jax.sharding import PartitionSpec as P

momentum_decay = 0.9
outer_rate = 0.7
highest = lax.Precision.HIGHEST


def on_device(inner_params, route, owner, outer_state, momentum):
    devices = lax.axis_size(("group", "path"))
    rank = lax.axis_index(("group", "path"))
    paths_dev = inner_params.shape[0]
    width = inner_params.shape[2]
    modules = owner.shape[1]
    labels = jnp.arange(modules, dtype=jnp.int32)
    all_hot = (route[:, :, None] == labels[None, None, :]).astype(jnp.float32)
    counts = jnp.sum(all_hot, axis=0).reshape(2 * modules)
    own_route = lax.dynamic_slice_in_dim(route, rank * paths_dev, paths_dev, 0)
    own_hot = (own_route[:, :, None] == labels[None, None, :]).astype(jnp.float32)
    level_mask = jnp.eye(2, dtype=jnp.float32)
    path_hot = jnp.einsum("plm,lk->plkm", own_hot, level_mask).reshape(paths_dev * 2, 2 * modules)
    flat_params = inner_params.reshape(paths_dev * 2, width)
    module_part = jnp.dot(path_hot.T, flat_params, precision=highest)
    slot_ids = jnp.arange(devices, dtype=jnp.int32)
    slot_hot = (owner.reshape(-1)[None, :] == slot_ids[:, None]).astype(jnp.float32)
    my_hot = lax.dynamic_slice_in_dim(slot_hot, rank, 1, 0)
    owned = jnp.sum(my_hot) > 0.5
    my_count = jnp.where(owned, jnp.dot(my_hot, counts, precision=highest), 1.0)
    rows_hot = slot_hot
    totals = lax.psum_scatter(
        jnp.dot(rows_hot, module_part, precision=highest),
        ("group", "path"),
        scatter_dimension=0,
        tiled=True,
    )
    delta = outer_state - totals / my_count[:, None]
    fresh_momentum = momentum_decay * momentum + delta
    fresh = outer_state - outer_rate * (delta + momentum_decay * fresh_momentum)
    new_momentum = jnp.where(owned, fresh_momentum, momentum)
    rows_hot = slot_hot
    module_fresh = jnp.dot(
        rows_hot.T, lax.all_gather(fresh, ("group", "path"), axis=0, tiled=True), precision=highest
    )
    snapshots = jnp.dot(path_hot, module_fresh, precision=highest)
    return (snapshots.reshape(paths_dev, 2, width), new_momentum)


def solution(mesh):
    return jax.shard_map(
        on_device,
        mesh=mesh,
        in_specs=(
            P(("group", "path"), None, None),
            P(),
            P(),
            P(("group", "path"), None),
            P(("group", "path"), None),
        ),
        out_specs=(P(("group", "path"), None, None), P(("group", "path"), None)),
        check_vma=False,
    )
```

profile of v0, /device:TPU:1, one launch (start us, length us, event | category | flops | bytes accessed | tf_op | source)
XLA Modules:
  0.0 347.7 jit_solution(16402466085146405931)
XLA Ops:
  7.2 0.0 all-reduce.3.cloned.1.call-start
  7.2 0.8 constant_dynamic-slice_fusion.1
  8.0 0.1 copy.11
  8.1 0.1 fusion.5
  8.2 0.8 eq.48
  8.9 0.1 multiply_bitcast_fusion
  9.0 0.1 reshape.30
  9.1 1.5 reshape.31
  10.6 3.5 %fusion.7 = f32[32,32768]{1,0:T(8,128)S(1)} fusion(f32[4,32]{1,0:T(4,128)S(1)} %reshape.30, f32[4,32768]{1,0:T(4,128)S(1)} %reshape.31), kind=kOutput, calls=%fused_computation.22 | convolution fusion | flops 50331648 | bytes 4719104 | tf_op jit(solution)/shard_map/dot_general | solution.py:25
  14.1 9.4 %fusion.2 = f32[128,32768]{1,0:T(8,128)} fusion(f32[32,32768]{1,0:T(8,128)S(1)} %fusion.7, s32[32]{0:T(128)S(1)} %eq.48), kind=kOutput, calls=%fused_computation.8 | convolution fusion | flops 1610616832 | bytes 20971648 | tf_op jit(solution)/shard_map/dot_general | solution.py:33
  23.5 0.0 copy-start.2
  23.5 0.0 copy-start
  23.5 0.0 copy-start.1
  23.5 0.0 all-reduce.3.cloned.1.call-update
  23.5 0.2 all-gather.3.cloned.1.call-start
  23.7 0.4 copy-done.2
  24.1 0.1 convert_reduce_fusion
  24.2 0.1 reshape.33
  24.3 0.6 convert_reduce_fusion.1
  25.6 0.6 fusion.6
  26.9 216.8 %all-reduce.3.cloned.1.call-done = f32[128,32768]{1,0:T(8,128)} async-done(((f32[128,32768]{1,0:T(8,128)}), f32[128,32768]{1,0:T(8,128)}) %all-reduce.3.cloned.1.call-update) | async-done | bytes 16777232
  243.7 0.0 copy-done
  243.7 0.0 copy-done.1
  243.7 2.2 broadcast_select_fusion
  245.9 1.0 subtract_bitcast_fusion
  246.9 0.0 all-gather.3.cloned.1.call-update
  246.9 0.1 dot_general.27
  247.0 80.0 %all-gather.3.cloned.1.call-done = f32[128,1,32768]{2,1,0:T(1,128)} async-done(((f32[1,1,32768]{2,1,0:T(1,128)}), f32[128,1,32768]{2,1,0:T(1,128)}) %all-gather.3.cloned.1.call-update) | async-done | bytes 16777232 | tf_op jit(solution)/shard_map/all_gather | solution.py:44
  327.0 10.7 %convolution_bitcast_fusion = f32[32,32768,1]{1,0,2:T(8,128)S(1)} fusion(f32[128,1,32768]{2,1,0:T(1,128)} %all-gather.3.cloned.1.call-done, s32[32]{0:T(128)S(1)} %eq.48), kind=kOutput, calls=%fused_computation | convolution fusion | flops 1610616832 | bytes 20971648 | tf_op jit(solution)/shard_map/dot_general | solution.py:43
  337.7 3.1 fusion.8
  (2 shorter events, 0.0 us)
Async XLA Ops:
  7.2 236.5 %all-reduce.3.cloned.1.call-start = ((), (), s32[]{:S(2)}) async-start(), calls=%async_computation.1 | async-start | bytes 33554432
  23.5 0.7 copy-start.2
  23.5 220.2 %copy-start = (f32[1,32768]{1,0:T(1,128)S(1)}, f32[1,32768]{1,0:T(1,128)}, u32[]{:S(2)}) copy-start(f32[1,32768]{1,0:T(1,128)} %param.8) | copy-start | bytes 393220
  23.5 220.2 %copy-start.1 = (f32[1,32768]{1,0:T(1,128)S(1)}, f32[1,32768]{1,0:T(1,128)}, u32[]{:S(2)}) copy-start(f32[1,32768]{1,0:T(1,128)} %param.9) | copy-start | bytes 393220
  23.5 303.5 %all-gather.3.cloned.1.call-start = ((), (), s32[]{:S(2)}) async-start(), calls=%async_computation | async-start | bytes 16908288 | tf_op jit(solution)/shard_map/all_gather | solution.py:44
Sparse Core Ops, SparseCore 0:
  23.6 220.0 all-reduce.2
  247.9 79.0 all-gather.2
where the time goes:
time: 348 us
  waiting for transfers between devices  297 us (85%)
  matrix products  26.8 us (8%)
  between operations  15.4 us (4%)
  other arithmetic  4.62 us (1%)
  local copies, waits for them, and re-layouts  3.78 us (1%)
    unnamed x3, waiting for transfers between devices  217 us
    all_gather x1, waiting for transfers between devices, on_device(): lax.all_gather(fresh, ('group', 'path'), axis=0, tiled=True)  80 us
    dot_general x1, matrix products, on_device(): jnp.dot(rows_hot.T, lax.all_gather(fresh, ('group', 'path'), axis=0, tile...  10.7 us
    dot_general x1, matrix products, on_device(): jnp.dot(rows_hot, module_part, precision=highest)  9.39 us
  transfers between devices with their start and end apart: 2, of which 2 were waited for; matrix products, arithmetic and copies ran while one was open for 0% of the time, Pallas kernels for 0%

commit v1 on v0

v1 whole, which is shorter than its diff:
```python
import jax
import jax.numpy as jnp
from jax import lax
from jax.sharding import PartitionSpec as P

momentum_decay = 0.9
outer_rate = 0.7
highest = lax.Precision.HIGHEST
axes = ("group", "path")


def on_device(inner_params, route, owner, outer_state, momentum):
    devices = lax.axis_size(axes)
    rank = lax.axis_index(axes)
    paths_dev = inner_params.shape[0]
    width = inner_params.shape[2]
    modules = owner.shape[1]
    rows = 2 * paths_dev
    chunk = width // devices
    labels = jnp.arange(modules, dtype=jnp.int32)
    hot = (route[:, :, None] == labels).astype(jnp.float32)
    counts = jnp.sum(hot, axis=0).reshape(2 * modules, 1)
    path_hot = (hot[:, :, None, :] * jnp.eye(2, dtype=jnp.float32)[None, :, :, None]).reshape(-1, 2 * modules)
    own_hot = (owner.reshape(1, -1) == jnp.arange(devices, dtype=jnp.int32)[:, None]).astype(jnp.float32)
    step = outer_rate * (1 + momentum_decay)
    own = (1 - step) * outer_state - outer_rate * momentum_decay * momentum_decay * momentum
    send = jnp.concatenate([inner_params.reshape(rows, width), own], axis=0)
    send = send.reshape(rows + 1, devices, chunk).transpose(1, 0, 2)
    got = lax.all_to_all(send, axes, 0, 0, tiled=True)
    got_paths = got[:, :rows].reshape(devices * rows, chunk)
    mean = jnp.dot(path_hot.T, got_paths, precision=highest) / counts
    fresh = step * mean + jnp.dot(own_hot.T, got[:, rows], precision=highest)
    back_paths = jnp.dot(path_hot, fresh, precision=highest).reshape(devices, rows, chunk)
    back_own = jnp.dot(own_hot, mean, precision=highest).reshape(devices, 1, chunk)
    back = lax.all_to_all(jnp.concatenate([back_paths, back_own], axis=1), axes, 0, 0, tiled=True)
    back = back.transpose(1, 0, 2).reshape(rows + 1, width)
    owned = jnp.any(owner == rank)
    delta = outer_state - back[rows:]
    new_momentum = jnp.where(owned, momentum_decay * momentum + delta, momentum)
    return back[:rows].reshape(paths_dev, 2, width), new_momentum


def solution(mesh):
    rows = P(axes, None)
    return jax.shard_map(
        on_device,
        mesh=mesh,
        in_specs=(P(axes, None, None), P(), P(), rows, rows),
        out_specs=(P(axes, None, None), rows),
        check_vma=False,
    )
```

time: 348 us -> 65.8 us (0.19)
  waiting for transfers between devices: 297 us -> 35.8 us
  matrix products: 26.8 us -> 1.52 us
  starting transfers between devices: 0.26 us -> 15.7 us
  between operations: 15.4 us -> 0.82 us
    unnamed x3 -> x0, waiting for transfers between devices: 217 us -> none
    all_gather x1 -> x0, waiting for transfers between devices: 80 us -> none  [on_device(): lax.all_gather(fresh, ('group', 'path'), axis=0, tiled=True)]
    all_to_all x0 -> x2, waiting for transfers between devices: none -> 35.8 us  [the longest x1 18.7 us: on_device(): lax.all_to_all(jnp.concatenate([back_paths, back_own], axis=1), axes, 0,...]
    dot_general x4, matrix products: 26.8 us -> 1.52 us  [the longest x1 0.56 us: on_device(): mean = jnp.dot(path_hot.T, got_paths, precision=highest) / counts]
    all_to_all x0 -> x2, starting transfers between devices: none -> 15.7 us  [the longest x1 11.5 us: on_device(): got = lax.all_to_all(send, axes, 0, 0, tiled=True)]
  transfers between devices with their start and end apart: 2 -> 2, of which waited for: 2 -> 2; matrix products, arithmetic and copies ran while one was open for 0% -> 4% of each run, Pallas kernels for 0% -> 0%
where the time goes in v1:
time: 65.8 us; the launch traced here: 65.4 us
  waiting for transfers between devices  35.8 us (54%)
  starting transfers between devices  15.7 us (24%)
  local copies, waits for them, and re-layouts  6.98 us (11%)
  other arithmetic  4.6 us (7%)
  matrix products  1.52 us (2%)
  between operations  0.82 us (1%)
    all_to_all x1, waiting for transfers between devices, on_device(): lax.all_to_all(jnp.concatenate([back_paths, back_own], axis=1), axes, 0,...  18.7 us
    all_to_all x1, waiting for transfers between devices, on_device(): got = lax.all_to_all(send, axes, 0, 0, tiled=True)  17 us
    all_to_all x1, starting transfers between devices, on_device(): got = lax.all_to_all(send, axes, 0, 0, tiled=True)  11.5 us
    all_to_all x1, starting transfers between devices, on_device(): lax.all_to_all(jnp.concatenate([back_paths, back_own], axis=1), axes, 0,...  4.25 us
    concatenate x2, local copies, waits for them, and re-layouts, on_device(): send = jnp.concatenate([inner_params.reshape(rows, width), own], axis=0)  1.83 us
    select_n x1, other arithmetic, on_device(): new_momentum = jnp.where(owned, momentum_decay * momentum + delta, momentum)  1.51 us
    concatenate x1, local copies, waits for them, and re-layouts, on_device(): jnp.concatenate([back_paths, back_own], axis=1)  1.38 us
  transfers between devices with their start and end apart: 2, of which 2 were waited for; matrix products, arithmetic and copies ran while one was open for 4% of the time, Pallas kernels for 0%

profile of v1, /device:TPU:1, one launch (start us, length us, event | category | flops | bytes accessed | tf_op | source)
XLA Modules:
  0.0 65.4 jit_solution(17292508999021508381)
XLA Ops:
  0.6 1.5 %concatenate.11 = f32[4,128,256]{2,1,0:T(8,128)S(1)} reshape(f32[2,2,32768]{2,1,0:T(2,128)} %param.5) | data formatting | bytes 1048576 | tf_op jit(solution)/shard_map/concatenate | solution.py:27
  2.1 0.0 copy-start
  2.1 0.0 copy-start.1
  2.1 0.3 copy.18
  2.5 0.5 copy-done
  3.0 0.1 copy-done.1
  3.1 0.2 multiply_subtract_fusion
  3.3 1.2 %maximum_bitcast_fusion = f32[128,5,256]{2,1,0:T(8,128)} fusion(f32[1,128,256]{2,0,1:T(1,128)S(1)} %bitcast.19, f32[4,128,256]{2,0,1:T(4,128)S(1)} %copy.18), kind=kLoop, calls=%fused_computation.4 | loop fusion | flops 163840 | bytes 1310720 | tf_op jit(solution)/shard_map/transpose | solution.py:28
  4.5 0.0 copy-start.2
  4.5 11.5 %all-to-all-start = ((f32[128,5,256]{2,1,0:T(8,128)}), f32[128,5,256]{2,1,0:T(8,128)S(1)}, u32[]{:S(2)}, u32[]{:S(2)}) async-start(f32[128,5,256]{2,1,0:T(8,128)} %maximum_bitcast_fusion), calls=%async_computation | async-start | bytes 2097152 | tf_op jit(solution)/shard_map/all_to_all | solution.py:29
  16.0 0.0 copy-done.2
  16.0 0.1 copy.17
  16.2 0.3 compare_convert_fusion
  16.5 0.2 broadcast_multiply_fusion
  16.8 0.3 mul.58
  17.1 0.0 copy-start.3
  17.1 0.4 mul.57
  17.5 0.3 copy-done.3
  17.8 0.1 eq.49
  17.8 0.3 fusion.7
  18.2 0.1 div.10
  18.3 17.0 %all-to-all-done = f32[128,5,256]{2,1,0:T(8,128)S(1)} async-done(((f32[128,5,256]{2,1,0:T(8,128)}), f32[128,5,256]{2,1,0:T(8,128)S(1)}, u32[]{:S(2)}, u32[]{:S(2)}) %all-to-all-start) | async-done | bytes 655392 | tf_op jit(solution)/shard_map/all_to_all | solution.py:29
  35.3 0.1 slice.21
  35.4 0.2 reshape.57
  35.6 0.6 convolution_divide_fusion
  36.2 0.2 convolution_bitcast_fusion
  36.4 0.1 slice.22
  36.5 0.2 fusion
  36.7 0.5 fusion.1
  37.3 1.4 %copy.21 = f32[128,5,256]{2,1,0:T(8,128)} copy(f32[128,5,256]{2,0,1:T(8,128)S(1)} %pad_maximum_fusion) | data formatting | bytes 1310720 | tf_op jit(solution)/shard_map/concatenate | solution.py:35
  38.7 4.2 %all-to-all-start.1 = ((f32[128,5,256]{2,1,0:T(8,128)}), f32[128,5,256]{2,1,0:T(8,128)S(1)}, u32[]{:S(2)}, u32[]{:S(2)}) async-start(f32[128,5,256]{2,1,0:T(8,128)} %copy.21), calls=%async_computation.1 | async-start | bytes 2097152 | tf_op jit(solution)/shard_map/all_to_all | solution.py:35
  43.0 0.7 %compare_reduce_fusion = pred[]{:T(512)} fusion(s32[2,16]{1,0:T(2,128)S(1)} %copy-done.3, s32[]{:T(128)S(6)} %add.10), kind=kLoop, calls=%fused_computation.17 | loop fusion | flops 63 | bytes 133 | tf_op jit(solution)/shard_map/reduce_or | solution.py:37
  43.7 18.7 %all-to-all-done.1 = f32[128,5,256]{2,1,0:T(8,128)S(1)} async-done(((f32[128,5,256]{2,1,0:T(8,128)}), f32[128,5,256]{2,1,0:T(8,128)S(1)}, u32[]{:S(2)}, u32[]{:S(2)}) %all-to-all-start.1) | async-done | bytes 655392 | tf_op jit(solution)/shard_map/all_to_all | solution.py:35
  62.4 0.1 slice.24
  62.5 0.1 slice.23
  62.6 0.1 copy.22
  62.8 1.1 %reshape.59 = f32[2,2,32768]{2,1,0:T(2,128)} reshape(f32[4,128,256]{2,1,0:T(8,128)S(1)} %copy.22) | data formatting | bytes 1048576 | tf_op jit(solution)/shard_map/reshape | solution.py:40
  63.9 1.5 %broadcast_select_fusion = f32[1,32768]{1,0:T(1,128)} fusion(f32[1,32768]{1,0:T(1,128)S(1)} %copy-done, pred[]{:T(512)} %compare_reduce_fusion, f32[1,32768]{1,0:T(1,128)S(1)} %copy-done.1, f32[1,32768]{1,0:T(1,128)S(1)} %bitcast.18), kind=kLoop, calls=%fused_computation.10 | loop fusion | flops 131072 | bytes 524289 | tf_op jit(solution)/shard_map/jit(_where)/select_n | solution.py:39
  (2 shorter events, 0.1 us)
Async XLA Ops:
  2.1 0.9 %copy-start = (f32[1,32768]{1,0:T(1,128)S(1)}, f32[1,32768]{1,0:T(1,128)}, u32[]{:S(2)}) copy-start(f32[1,32768]{1,0:T(1,128)} %param.9) | copy-start | bytes 393220
  2.1 1.0 %copy-start.1 = (f32[1,32768]{1,0:T(1,128)S(1)}, f32[1,32768]{1,0:T(1,128)}, u32[]{:S(2)}) copy-start(f32[1,32768]{1,0:T(1,128)} %param.8) | copy-start | bytes 393220
  4.5 11.5 %copy-start.2 = (s32[256,2]{0,1:T(2,128)S(1)}, s32[256,2]{0,1:T(2,128)}, u32[]{:S(2)}) copy-start(s32[256,2]{0,1:T(2,128)} %param.6) | copy-start | bytes 6148
  4.5 30.8 %all-to-all-start = ((f32[128,5,256]{2,1,0:T(8,128)}), f32[128,5,256]{2,1,0:T(8,128)S(1)}, u32[]{:S(2)}, u32[]{:S(2)}) async-start(f32[128,5,256]{2,1,0:T(8,128)} %maximum_bitcast_fusion), calls=%async_computation | async-start | bytes 2097152 | tf_op jit(solution)/shard_map/all_to_all | solution.py:29
  17.1 0.7 %copy-start.3 = (s32[2,16]{1,0:T(2,128)S(1)}, s32[2,16]{1,0:T(2,128)}, u32[]{:S(2)}) copy-start(s32[2,16]{1,0:T(2,128)} %param.7) | copy-start | bytes 388
  38.7 23.7 %all-to-all-start.1 = ((f32[128,5,256]{2,1,0:T(8,128)}), f32[128,5,256]{2,1,0:T(8,128)S(1)}, u32[]{:S(2)}, u32[]{:S(2)}) async-start(f32[128,5,256]{2,1,0:T(8,128)} %copy.21), calls=%async_computation.1 | async-start | bytes 2097152 | tf_op jit(solution)/shard_map/all_to_all | solution.py:35

commit v2 on v1

v2 whole, which is shorter than its diff:
```python
import functools

import jax
import jax.numpy as jnp
from jax import lax
from jax.experimental import pallas as pl
from jax.experimental.pallas import tpu as pltpu
from jax.sharding import PartitionSpec as P

axes = ("group", "path")
momentum_decay = 0.9
outer_rate = 0.7
step = outer_rate * (1 + momentum_decay)
MESH = pl.DeviceIdType.MESH
f32 = jnp.float32
bf16 = jnp.bfloat16


def split(x):
    high = x.astype(bf16)
    return high, (x - high.astype(f32)).astype(bf16)


def peer(s, group, path):
    s = lax.rem(s * 37, 128)
    core = lax.rem(lax.rem(group, 2) + s // 64, 2)
    y = lax.rem(group // 2 + lax.rem(s // 16, 4), 4)
    z = lax.rem(path // 4 + lax.rem(s // 4, 4), 4)
    x = lax.rem(lax.rem(path, 4) + lax.rem(s, 4), 4)
    return y * 2 + core, z * 4 + x


def kernel(n, x_ref, route_ref, owner_ref, outer_ref, mom_ref, back_ref, newm_ref,
           own_ref, got_ref, gotown_ref, res_ref, resown_ref, backown_ref,
           send_sem, recv_sem, sendown_sem, recvown_sem, send2_sem, recv2_sem, sendown2_sem, recvown2_sem):
    group, path = lax.axis_index("group"), lax.axis_index("path")
    me = group * 16 + path
    barrier = pltpu.get_barrier_semaphore()

    @pl.loop(1, n)
    def _(s):
        pl.semaphore_signal(barrier, inc=1, device_id=peer(s, group, path), device_id_type=MESH)

    own_ref[...] = (1 - step) * outer_ref[...] - (outer_rate * momentum_decay * momentum_decay) * mom_ref[...]
    pl.semaphore_wait(barrier, n - 1)

    def exchange(src, dst, own_src, own_dst, s1, r1, s2, r2):
        local = pltpu.make_async_copy(src(me), dst(me), r1)
        local.start()
        local2 = pltpu.make_async_copy(own_src(me), own_dst(me), r2)
        local2.start()

        @pl.loop(1, n)
        def _(s):
            to = peer(s, group, path)
            rank = to[0] * 16 + to[1]
            pltpu.make_async_remote_copy(src(rank), dst(me), s1, r1, device_id=to, device_id_type=MESH).start()
            pltpu.make_async_remote_copy(own_src(rank), own_dst(me), s2, r2, device_id=to, device_id_type=MESH).start()

    exchange(lambda r: x_ref.at[:, r], lambda r: got_ref.at[r], lambda r: own_ref.at[r], lambda r: gotown_ref.at[r],
             send_sem, recv_sem, sendown_sem, recvown_sem)
    rows = 8 * n
    route = route_ref[...].astype(bf16)
    k = lax.broadcasted_iota(jnp.int32, (2 * n, rows), 1) // 4
    p = lax.broadcasted_iota(jnp.int32, (2 * n, rows), 0)
    spread = (k == p).astype(f32).astype(bf16)
    both = jnp.dot(route, spread, preferred_element_type=f32)
    col = lax.broadcasted_iota(jnp.int32, (1, rows), 1)
    label = jnp.where(lax.rem(col, 2) == 0, both[0:1], both[1:2]).astype(jnp.int32) + 16 * lax.rem(col, 4)
    hot = (label == lax.broadcasted_iota(jnp.int32, (64, rows), 0)).astype(f32)
    counts = jnp.sum(hot, axis=1, keepdims=True)
    hot2 = jnp.concatenate([hot, hot], axis=0).T.astype(bf16)
    hot = hot.astype(bf16)
    r = lax.broadcasted_iota(jnp.int32, (64, 16), 0)
    owners = owner_ref[...]
    table = jnp.where(lax.rem(r // 16, 2) == 0, owners[0:1], owners[1:2])
    pick = lax.rem(r, 16) == lax.broadcasted_iota(jnp.int32, (64, 16), 1)
    owner_col = jnp.sum(jnp.where(pick, table, 0).astype(f32), axis=1, keepdims=True).astype(jnp.int32)
    k = lax.broadcasted_iota(jnp.int32, (64, 2 * n), 1)
    tile = lax.broadcasted_iota(jnp.int32, (64, 2 * n), 0) // 32
    own_hot = jnp.logical_and(owner_col == k // 2, tile == lax.rem(k, 2)).astype(f32)
    own_hot2 = jnp.concatenate([own_hot, own_hot], axis=0).T.astype(bf16)
    own_hot = own_hot.astype(bf16)
    owned = jnp.sum((owners == me).astype(f32)) > 0.5

    def finish(s, r, ref, out):
        pltpu.make_async_copy(ref, ref, r).wait()
        part = out
        pltpu.make_async_copy(part, part, s).wait()

    pltpu.make_async_copy(got_ref, got_ref, recv_sem).wait()
    pltpu.make_async_copy(gotown_ref, gotown_ref, recvown_sem).wait()
    high, low = split(got_ref[...].reshape(rows, 128))
    mean = jnp.dot(hot, high, preferred_element_type=f32) + jnp.dot(hot, low, preferred_element_type=f32)
    mean = mean / counts
    high, low = split(gotown_ref[...].reshape(2 * n, 128))
    fresh = step * mean + (
        jnp.dot(own_hot, high, preferred_element_type=f32) + jnp.dot(own_hot, low, preferred_element_type=f32))
    res_ref[...] = jnp.dot(hot2, jnp.concatenate(split(fresh), axis=0), preferred_element_type=f32).reshape(res_ref.shape)
    resown_ref[...] = jnp.dot(own_hot2, jnp.concatenate(split(mean), axis=0), preferred_element_type=f32).reshape(resown_ref.shape)
    exchange(lambda r: res_ref.at[r], lambda r: back_ref.at[r], lambda r: resown_ref.at[r], lambda r: backown_ref.at[r],
             send2_sem, recv2_sem, sendown2_sem, recvown2_sem)
    pltpu.make_async_copy(backown_ref, backown_ref, recvown2_sem).wait()
    delta = outer_ref[...] - backown_ref[...]
    newm_ref[...] = jnp.where(owned, momentum_decay * mom_ref[...] + delta, mom_ref[...])
    pltpu.make_async_copy(back_ref, back_ref, recv2_sem).wait()
    last = got_ref.at[pl.ds(0, n - 1)]
    lastown = gotown_ref.at[pl.ds(0, n - 1)]
    pltpu.make_async_copy(last, last, send_sem).wait()
    pltpu.make_async_copy(lastown, lastown, sendown_sem).wait()
    pltpu.make_async_copy(last, last, send2_sem).wait()
    pltpu.make_async_copy(lastown, lastown, sendown2_sem).wait()


def on_device(inner_params, route, owner, outer_state, momentum):
    n = lax.axis_size(axes)
    x = inner_params.reshape(2, 2, n, 2, 128).transpose(0, 2, 3, 1, 4).reshape(2, n, 4, 128)
    vmem = pl.BlockSpec(memory_space=pltpu.VMEM)
    back, newm = pl.pallas_call(
        functools.partial(kernel, n),
        out_shape=(jax.ShapeDtypeStruct((n, 2, 4, 128), f32), jax.ShapeDtypeStruct((n, 2, 128), f32)),
        in_specs=[vmem] * 5,
        out_specs=(vmem, vmem),
        scratch_shapes=[
            pltpu.VMEM((n, 2, 128), f32),
            pltpu.VMEM((n, 2, 4, 128), f32),
            pltpu.VMEM((n, 2, 128), f32),
            pltpu.VMEM((n, 2, 4, 128), f32),
            pltpu.VMEM((n, 2, 128), f32),
            pltpu.VMEM((n, 2, 128), f32),
        ] + [pltpu.SemaphoreType.DMA] * 8,
        compiler_params=pltpu.CompilerParams(collective_id=0, has_side_effects=True, vmem_limit_bytes=40 * 2**20),
    )(x, route.T, owner, outer_state.reshape(n, 2, 128), momentum.reshape(n, 2, 128))
    out = back.reshape(n, 2, 2, 2, 128).transpose(1, 3, 0, 2, 4).reshape(inner_params.shape)
    return out, newm.reshape(momentum.shape)


def solution(mesh):
    rows = P(axes, None)
    return jax.shard_map(
        on_device,
        mesh=mesh,
        in_specs=(P(axes, None, None), P(), P(), rows, rows),
        out_specs=(P(axes, None, None), rows),
        check_vma=False,
    )
```

time: 65.8 us -> 45 us (0.68)
  Pallas kernels: 0 us -> 38.2 us
  waiting for transfers between devices: 35.8 us -> 0 us
  starting transfers between devices: 15.7 us -> 0 us
  other arithmetic: 4.6 us -> 0 us
  matrix products: 1.52 us -> 0 us
  local copies, waits for them, and re-layouts: 6.98 us -> 5.85 us
    pallas_call x0 -> x1, Pallas kernels: none -> 38.2 us  [on_device(): pl.pallas_call(functools.partial(kernel, n), out_shape=(jax.ShapeDtypeStr...]
    all_to_all x2 -> x0, waiting for transfers between devices: 35.8 us -> none  [the longest x1 18.7 us: on_device(): lax.all_to_all(jnp.concatenate([back_paths, back_own], axis=1), axes, 0,...]
    all_to_all x2 -> x0, starting transfers between devices: 15.7 us -> none  [the longest x1 11.5 us: on_device(): got = lax.all_to_all(send, axes, 0, 0, tiled=True)]
    concatenate x3 -> x0, local copies, waits for them, and re-layouts: 3.21 us -> none  [the longest x2 1.83 us: on_device(): send = jnp.concatenate([inner_params.reshape(rows, width), own], axis=0)]
    unnamed x9 -> x11, local copies, waits for them, and re-layouts: 1.03 us -> 4.18 us
    dot_general x4 -> x0, matrix products: 1.52 us -> none  [the longest x1 0.56 us: on_device(): mean = jnp.dot(path_hot.T, got_paths, precision=highest) / counts]
    select_n x1 -> x0, other arithmetic: 1.51 us -> none  [on_device(): new_momentum = jnp.where(owned, momentum_decay * momentum + delta, momentum)]
    transpose x1 -> x0, other arithmetic: 1.18 us -> none  [on_device(): send = send.reshape(rows + 1, devices, chunk).transpose(1, 0, 2)]
  transfers between devices with their start and end apart: 2 -> 0, of which waited for: 2 -> 0; matrix products, arithmetic and copies ran while one was open for 4% -> 0% of each run, Pallas kernels for 0% -> 0%
where the time goes in v2:
time: 45 us; the launch traced here: 44.8 us
  Pallas kernels  38.2 us (85%)
  local copies, waits for them, and re-layouts  5.85 us (13%)
  between operations  0.67 us (1%)
    pallas_call x1, Pallas kernels, on_device(): pl.pallas_call(functools.partial(kernel, n), out_shape=(jax.ShapeDtypeStr...  38.2 us
    unnamed x11, local copies, waits for them, and re-layouts  4.18 us
    reshape x1, local copies, waits for them, and re-layouts, on_device(): back.reshape(n, 2, 2, 2, 128).transpose(1, 3, 0, 2, 4)  1.39 us

profile of v2, /device:TPU:1, one launch (start us, length us, event | category | flops | bytes accessed | tf_op | source)
XLA Modules:
  0.0 44.8 jit_solution(8625412639851605285)
XLA Ops:
  0.6 0.0 copy-start.3
  0.6 0.0 copy-start.4
  0.7 0.7 %copy-done.3 = s32[256,2]{0,1:T(2,128)S(1)} copy-done((s32[256,2]{0,1:T(2,128)S(1)}, s32[256,2]{0,1:T(2,128)}, u32[]{:S(2)}) %copy-start.3) | copy-done | bytes 2072
  1.3 0.0 copy-done.4
  1.3 0.0 copy-start
  1.3 1.0 %copy-done = f32[2,2,32768]{2,1,0:T(2,128)S(1)} copy-done((f32[2,2,32768]{2,1,0:T(2,128)S(1)}, f32[2,2,32768]{2,1,0:T(2,128)}, u32[]{:S(2)}) %copy-start) | copy-done | bytes 524312
  2.4 0.0 copy-start.1
  2.4 0.9 %copy-done.1 = f32[1,32768]{1,0:T(1,128)S(1)} copy-done((f32[1,32768]{1,0:T(1,128)S(1)}, f32[1,32768]{1,0:T(1,128)}, u32[]{:S(2)}) %copy-start.1) | copy-done | bytes 131096
  3.3 0.0 copy-start.2
  3.3 0.9 %copy-done.2 = f32[1,32768]{1,0:T(1,128)S(1)} copy-done((f32[1,32768]{1,0:T(1,128)S(1)}, f32[1,32768]{1,0:T(1,128)}, u32[]{:S(2)}) %copy-start.2) | copy-done | bytes 131096
  4.2 38.2 %shard_map.68 = (f32[128,2,4,128]{3,2,1,0:T(4,128)S(1)}, f32[128,2,128]{2,1,0:T(2,128)S(1)}) custom-call(f32[2,128,4,128]{3,2,1,0:T(4,128)S(1)} %bitcast.12, s32[2,256]{1,0:T(2,128)S(1)} %bitcast.17, s32[2,16]{1,0:T(2,128)S(1)} %copy-done.4, f32[128,2,128]{2,1,0:T(2,128)S(1)} %bitcast.15, f32[128,2,128]{2,1,0:T(2,128)S(1)} %bitcast.16), custom_call_target="tpu_custom_call" | custom-call | tf_op jit(solution)/shard_map/pallas_call | solution.py:119
  42.4 0.3 copy.8
  42.7 1.4 %reshape.30 = f32[2,2,32768]{2,1,0:T(2,128)} reshape(f32[2,2,128,2,128]{4,3,2,1,0:T(2,128)S(1)} %copy.8) | data formatting | bytes 1048576 | tf_op jit(solution)/shard_map/reshape | solution.py:134
  44.1 0.7 %copy.10 = f32[1,32768]{1,0:T(1,128)} copy(f32[1,32768]{1,0:T(1,128)S(1)} %bitcast.14) | data formatting | bytes 262144
Async XLA Ops:
  0.6 0.7 %copy-start.3 = (s32[256,2]{0,1:T(2,128)S(1)}, s32[256,2]{0,1:T(2,128)}, u32[]{:S(2)}) copy-start(s32[256,2]{0,1:T(2,128)} %param.6) | copy-start | bytes 6148
  0.6 0.7 %copy-start.4 = (s32[2,16]{1,0:T(2,128)S(1)}, s32[2,16]{1,0:T(2,128)}, u32[]{:S(2)}) copy-start(s32[2,16]{1,0:T(2,128)} %owner_ref.1) | copy-start | bytes 388
  1.3 1.0 %copy-start = (f32[2,2,32768]{2,1,0:T(2,128)S(1)}, f32[2,2,32768]{2,1,0:T(2,128)}, u32[]{:S(2)}) copy-start(f32[2,2,32768]{2,1,0:T(2,128)} %param.5) | copy-start | bytes 1572868
  2.4 0.9 %copy-start.1 = (f32[1,32768]{1,0:T(1,128)S(1)}, f32[1,32768]{1,0:T(1,128)}, u32[]{:S(2)}) copy-start(f32[1,32768]{1,0:T(1,128)} %param.8) | copy-start | bytes 393220
  3.3 0.9 %copy-start.2 = (f32[1,32768]{1,0:T(1,128)S(1)}, f32[1,32768]{1,0:T(1,128)}, u32[]{:S(2)}) copy-start(f32[1,32768]{1,0:T(1,128)} %param.9) | copy-start | bytes 393220

commit v3 on v2

--- a/solution.py
+++ b/solution.py
@@ -22,25 +22,31 @@
 
 
 def peer(s, group, path):
-    s = lax.rem(s * 37, 128)
-    core = lax.rem(lax.rem(group, 2) + s // 64, 2)
-    y = lax.rem(group // 2 + lax.rem(s // 16, 4), 4)
-    z = lax.rem(path // 4 + lax.rem(s // 4, 4), 4)
-    x = lax.rem(lax.rem(path, 4) + lax.rem(s, 4), 4)
+    core = ((group & 1) + (s >> 6)) & 1
+    y = ((group >> 1) + ((s >> 4) & 3)) & 3
+    z = ((path >> 2) + ((s >> 2) & 3)) & 3
+    x = ((path & 3) + (s & 3)) & 3
     return y * 2 + core, z * 4 + x
 
 
-def kernel(n, x_ref, route_ref, owner_ref, outer_ref, mom_ref, back_ref, newm_ref,
+def kernel(n, x_ref, route_hbm, owner_hbm, outer_hbm, mom_hbm, back_ref, newm_ref,
+           route_ref, owner_ref, outer_ref, mom_ref, load_sem,
            own_ref, got_ref, gotown_ref, res_ref, resown_ref, backown_ref,
            send_sem, recv_sem, sendown_sem, recvown_sem, send2_sem, recv2_sem, sendown2_sem, recvown2_sem):
     group, path = lax.axis_index("group"), lax.axis_index("path")
     me = group * 16 + path
     barrier = pltpu.get_barrier_semaphore()
 
-    @pl.loop(1, n)
+    @pl.loop(1, n, unroll=n - 1)
     def _(s):
         pl.semaphore_signal(barrier, inc=1, device_id=peer(s, group, path), device_id_type=MESH)
 
+    loads = [pltpu.make_async_copy(a, b, load_sem.at[i]) for i, (a, b) in enumerate(
+        [(outer_hbm, outer_ref), (mom_hbm, mom_ref), (route_hbm, route_ref), (owner_hbm, owner_ref)])]
+    for load in loads:
+        load.start()
+    for load in loads:
+        load.wait()
     own_ref[...] = (1 - step) * outer_ref[...] - (outer_rate * momentum_decay * momentum_decay) * mom_ref[...]
     pl.semaphore_wait(barrier, n - 1)
 
@@ -50,9 +56,9 @@
         local2 = pltpu.make_async_copy(own_src(me), own_dst(me), r2)
         local2.start()
 
-        @pl.loop(1, n)
+        @pl.loop(1, n, unroll=n - 1)
         def _(s):
-            to = peer(s, group, path)
+            to = peer((s * 37) & (n - 1), group, path)
             rank = to[0] * 16 + to[1]
             pltpu.make_async_remote_copy(src(rank), dst(me), s1, r1, device_id=to, device_id_type=MESH).start()
             pltpu.make_async_remote_copy(own_src(rank), own_dst(me), s2, r2, device_id=to, device_id_type=MESH).start()
@@ -83,11 +89,6 @@
     own_hot = own_hot.astype(bf16)
     owned = jnp.sum((owners == me).astype(f32)) > 0.5
 
-    def finish(s, r, ref, out):
-        pltpu.make_async_copy(ref, ref, r).wait()
-        part = out
-        pltpu.make_async_copy(part, part, s).wait()
-
     pltpu.make_async_copy(got_ref, got_ref, recv_sem).wait()
     pltpu.make_async_copy(gotown_ref, gotown_ref, recvown_sem).wait()
     high, low = split(got_ref[...].reshape(rows, 128))
@@ -98,7 +99,7 @@
         jnp.dot(own_hot, high, preferred_element_type=f32) + jnp.dot(own_hot, low, preferred_element_type=f32))
     res_ref[...] = jnp.dot(hot2, jnp.concatenate(split(fresh), axis=0), preferred_element_type=f32).reshape(res_ref.shape)
     resown_ref[...] = jnp.dot(own_hot2, jnp.concatenate(split(mean), axis=0), preferred_element_type=f32).reshape(resown_ref.shape)
-    exchange(lambda r: res_ref.at[r], lambda r: back_ref.at[r], lambda r: resown_ref.at[r], lambda r: backown_ref.at[r],
+    exchange(lambda r: res_ref.at[r], lambda r: back_ref.at[:, r], lambda r: resown_ref.at[r], lambda r: backown_ref.at[r],
              send2_sem, recv2_sem, sendown2_sem, recvown2_sem)
     pltpu.make_async_copy(backown_ref, backown_ref, recvown2_sem).wait()
     delta = outer_ref[...] - backown_ref[...]
@@ -118,10 +119,15 @@
     vmem = pl.BlockSpec(memory_space=pltpu.VMEM)
     back, newm = pl.pallas_call(
         functools.partial(kernel, n),
-        out_shape=(jax.ShapeDtypeStruct((n, 2, 4, 128), f32), jax.ShapeDtypeStruct((n, 2, 128), f32)),
-        in_specs=[vmem] * 5,
+        out_shape=(jax.ShapeDtypeStruct((2, n, 4, 128), f32), jax.ShapeDtypeStruct((n, 2, 128), f32)),
+        in_specs=[pl.BlockSpec(memory_space=pltpu.HBM)] * 5,
         out_specs=(vmem, vmem),
         scratch_shapes=[
+            pltpu.VMEM((2, 2 * n), jnp.int32),
+            pltpu.VMEM(owner.shape, jnp.int32),
+            pltpu.VMEM((n, 2, 128), f32),
+            pltpu.VMEM((n, 2, 128), f32),
+            pltpu.SemaphoreType.DMA((4,)),
             pltpu.VMEM((n, 2, 128), f32),
             pltpu.VMEM((n, 2, 4, 128), f32),
             pltpu.VMEM((n, 2, 128), f32),
@@ -129,9 +135,9 @@
             pltpu.VMEM((n, 2, 128), f32),
             pltpu.VMEM((n, 2, 128), f32),
         ] + [pltpu.SemaphoreType.DMA] * 8,
-        compiler_params=pltpu.CompilerParams(collective_id=0, has_side_effects=True, vmem_limit_bytes=40 * 2**20),
+        compiler_params=pltpu.CompilerParams(collective_id=0, has_side_effects=True, vmem_limit_bytes=56 * 2**20),
     )(x, route.T, owner, outer_state.reshape(n, 2, 128), momentum.reshape(n, 2, 128))
-    out = back.reshape(n, 2, 2, 2, 128).transpose(1, 3, 0, 2, 4).reshape(inner_params.shape)
+    out = back.reshape(2, n, 2, 2, 128).transpose(0, 3, 1, 2, 4).reshape(inner_params.shape)
     return out, newm.reshape(momentum.shape)
 
 

time: 45 us -> 39.2 us (0.87)
  local copies, waits for them, and re-layouts: 5.85 us -> 2.56 us
  Pallas kernels: 38.2 us -> 35.8 us
    pallas_call x1, Pallas kernels: 38.2 us -> 35.8 us  [on_device(): pl.pallas_call(functools.partial(kernel, n), out_shape=(jax.ShapeDtypeStr...]
    unnamed x11 -> x4, local copies, waits for them, and re-layouts: 4.18 us -> 2.56 us
    reshape x1 -> x0, local copies, waits for them, and re-layouts: 1.39 us -> none  [on_device(): back.reshape(n, 2, 2, 2, 128).transpose(1, 3, 0, 2, 4)]
where the time goes in v3:
time: 39.2 us; the launch traced here: 39 us
  Pallas kernels  35.8 us (91%)
  local copies, waits for them, and re-layouts  2.56 us (7%)
  between operations  0.65 us (2%)
    pallas_call x1, Pallas kernels, on_device(): pl.pallas_call(functools.partial(kernel, n), out_shape=(jax.ShapeDtypeStr...  35.8 us
    unnamed x4, local copies, waits for them, and re-layouts  2.56 us

profile of v3, /device:TPU:1, one launch (start us, length us, event | category | flops | bytes accessed | tf_op | source)
XLA Modules:
  0.0 39.0 jit_solution(14270031081078604940)
XLA Ops:
  0.6 35.8 %shard_map.68 = (f32[2,128,4,128]{3,2,1,0:T(4,128)}, f32[128,2,128]{2,1,0:T(2,128)}) custom-call(f32[2,128,4,128]{3,2,1,0:T(4,128)} %bitcast.14, s32[2,256]{1,0:T(2,128)} %bitcast.19, s32[2,16]{1,0:T(2,128)} %owner_hbm.1, f32[128,2,128]{2,1,0:T(2,128)} %bitcast.17, f32[128,2,128]{2,1,0:T(2,128)} %bitcast.18), custom_call_target="tpu_custom_call" | custom-call | tf_op jit(solution)/shard_map/pallas_call | solution.py:120
  36.4 0.0 copy-start
  36.4 1.9 %copy.11 = f32[2,2,32768]{2,1,0:T(2,128)} copy(f32[2,2,32768]{2,1,0:T(2,128)} %bitcast.15) | data formatting | bytes 1048576
  38.3 0.0 copy-done
  38.4 0.7 %copy.12 = f32[1,32768]{1,0:T(1,128)} copy(f32[1,32768]{1,0:T(1,128)S(1)} %bitcast.16) | data formatting | bytes 262144
Async XLA Ops:
  36.4 1.9 %copy-start = (f32[128,2,128]{2,1,0:T(2,128)S(1)}, f32[128,2,128]{2,1,0:T(2,128)}, u32[]{:S(2)}) copy-start(f32[128,2,128]{2,1,0:T(2,128)} %get-tuple-element.5) | copy-start | bytes 393220

commit v4 on v3

v4 whole, which is shorter than its diff:
```python
import functools

import jax
import jax.numpy as jnp
from jax import lax
from jax.experimental import pallas as pl
from jax.experimental.pallas import tpu as pltpu
from jax.sharding import PartitionSpec as P

axes = ("group", "path")
momentum_decay = 0.9
outer_rate = 0.7
step = outer_rate * (1 + momentum_decay)
MESH = pl.DeviceIdType.MESH
f32 = jnp.float32
bf16 = jnp.bfloat16


def split(x):
    high = x.astype(bf16)
    return high, (x - high.astype(f32)).astype(bf16)


def pick(hot, x):
    both = jnp.dot(hot, jnp.concatenate(split(x), axis=1), preferred_element_type=f32)
    return both[:, :128] + both[:, 128:]


def spread(hot2, x):
    return jnp.dot(hot2, jnp.concatenate(split(x), axis=0), preferred_element_type=f32)


def peer(s, group, path):
    core = ((group & 1) + (s >> 6)) & 1
    y = ((group >> 1) + ((s >> 4) & 3)) & 3
    z = ((path >> 2) + ((s >> 2) & 3)) & 3
    x = ((path & 3) + (s & 3)) & 3
    return y * 2 + core, z * 4 + x


def kernel(n, x_ref, route_hbm, owner_hbm, outer_hbm, mom_hbm, back_ref, newm_ref,
           route_ref, owner_ref, outer_ref, mom_ref, load_sem,
           own_ref, got_ref, gotown_ref, res_ref, resown_ref, backown_ref,
           send_sem, recv_sem, sendown_sem, recvown_sem, send2_sem, recv2_sem, sendown2_sem, recvown2_sem):
    group, path = lax.axis_index("group"), lax.axis_index("path")
    me = group * 16 + path
    loads = [pltpu.make_async_copy(a, b, load_sem.at[i]) for i, (a, b) in enumerate(
        [(outer_hbm, outer_ref), (mom_hbm, mom_ref), (route_hbm, route_ref), (owner_hbm, owner_ref)])]
    for load in loads:
        load.start()
    barrier = pltpu.get_barrier_semaphore()

    @pl.loop(1, n, unroll=n - 1)
    def _(s):
        pl.semaphore_signal(barrier, inc=1, device_id=peer(s, group, path), device_id_type=MESH)

    for load in loads:
        load.wait()
    own_ref[...] = (1 - step) * outer_ref[...] - (outer_rate * momentum_decay * momentum_decay) * mom_ref[...]
    pl.semaphore_wait(barrier, n - 1)

    def exchange(*moves):
        for src, dst, _, recv in moves:
            pltpu.make_async_copy(src(me), dst(me), recv).start()

        @pl.loop(1, n, unroll=n - 1)
        def _(s):
            to = peer((s * 37) & (n - 1), group, path)
            rank = to[0] * 16 + to[1]
            for src, dst, sent, recv in moves:
                pltpu.make_async_remote_copy(
                    src(rank), dst(me), sent, recv, device_id=to, device_id_type=MESH).start()

    for t in range(2):
        moves = [(lambda r: x_ref.at[:, r, t], lambda r: got_ref.at[t, r], send_sem.at[t], recv_sem.at[t])]
        if t == 0:
            moves.append((lambda r: own_ref.at[r], lambda r: gotown_ref.at[r], sendown_sem, recvown_sem))
        exchange(*moves)

    rows = 4 * n
    route = route_ref[...].astype(f32).astype(bf16)
    k = lax.broadcasted_iota(jnp.int32, (2 * n, rows), 1) >> 1
    p = lax.broadcasted_iota(jnp.int32, (2 * n, rows), 0)
    both = jnp.dot(route, (k == p).astype(f32).astype(bf16), preferred_element_type=f32)
    level = lax.broadcasted_iota(jnp.int32, (1, rows), 1) & 1
    label = jnp.where(level == 0, both[0:1], both[1:2]).astype(jnp.int32) + 16 * level
    hot = (label == lax.broadcasted_iota(jnp.int32, (32, rows), 0)).astype(f32)
    counts = jnp.sum(hot, axis=1, keepdims=True)
    hot2 = jnp.concatenate([hot, hot], axis=0).T.astype(bf16)
    hot = hot.astype(bf16)
    r = lax.broadcasted_iota(jnp.int32, (32, 16), 0)
    owners = owner_ref[...]
    table = jnp.where(r < 16, owners[0:1], owners[1:2])
    mine = (r & 15) == lax.broadcasted_iota(jnp.int32, (32, 16), 1)
    owner_col = jnp.sum(jnp.where(mine, table, 0).astype(f32), axis=1, keepdims=True).astype(jnp.int32)
    own_hot = (owner_col == lax.broadcasted_iota(jnp.int32, (32, n), 1)).astype(f32)
    own_hot2 = jnp.concatenate([own_hot, own_hot], axis=0).T.astype(bf16)
    own_hot = own_hot.astype(bf16)
    owned = jnp.sum((owners == me).astype(f32)) > 0.5

    for t in range(2):
        pltpu.make_async_copy(got_ref.at[t], got_ref.at[t], recv_sem.at[t]).wait()
        if t == 0:
            pltpu.make_async_copy(gotown_ref, gotown_ref, recvown_sem).wait()
        mean = pick(hot, got_ref[t].reshape(rows, 128)) / counts
        fresh = step * mean + pick(own_hot, gotown_ref[:, t, :])
        res_ref[t] = spread(hot2, fresh).reshape(res_ref.shape[1:])
        resown_ref[:, t, :] = spread(own_hot2, mean)
        moves = [(lambda r: res_ref.at[t, r], lambda r: back_ref.at[:, r, t], send2_sem.at[t], recv2_sem.at[t])]
        if t == 1:
            moves.append((lambda r: resown_ref.at[r], lambda r: backown_ref.at[r], sendown2_sem, recvown2_sem))
        exchange(*moves)
    pltpu.make_async_copy(backown_ref, backown_ref, recvown2_sem).wait()
    delta = outer_ref[...] - backown_ref[...]
    newm_ref[...] = jnp.where(owned, momentum_decay * mom_ref[...] + delta, mom_ref[...])
    for t in range(2):
        pltpu.make_async_copy(got_ref.at[t], got_ref.at[t], recv2_sem.at[t]).wait()
    last = got_ref.at[0, pl.ds(0, n - 1)]
    for sem in (send_sem, send2_sem):
        for t in range(2):
            pltpu.make_async_copy(last, last, sem.at[t]).wait()
    lastown = gotown_ref.at[pl.ds(0, n - 1)]
    pltpu.make_async_copy(lastown, lastown, sendown_sem).wait()
    pltpu.make_async_copy(lastown, lastown, sendown2_sem).wait()


def on_device(inner_params, route, owner, outer_state, momentum):
    n = lax.axis_size(axes)
    x = inner_params.reshape(2, 2, n, 2, 128).transpose(0, 2, 3, 1, 4)
    vmem = pl.BlockSpec(memory_space=pltpu.VMEM)
    one = pltpu.SemaphoreType.DMA
    two = pltpu.SemaphoreType.DMA((2,))
    back, newm = pl.pallas_call(
        functools.partial(kernel, n),
        out_shape=(jax.ShapeDtypeStruct((2, n, 2, 2, 128), f32), jax.ShapeDtypeStruct((n, 2, 128), f32)),
        in_specs=[pl.BlockSpec(memory_space=pltpu.HBM)] * 5,
        out_specs=(vmem, vmem),
        scratch_shapes=[
            pltpu.VMEM((2, 2 * n), jnp.int32),
            pltpu.VMEM(owner.shape, jnp.int32),
            pltpu.VMEM((n, 2, 128), f32),
            pltpu.VMEM((n, 2, 128), f32),
            pltpu.SemaphoreType.DMA((4,)),
            pltpu.VMEM((n, 2, 128), f32),
            pltpu.VMEM((2, n, 2, 2, 128), f32),
            pltpu.VMEM((n, 2, 128), f32),
            pltpu.VMEM((2, n, 2, 2, 128), f32),
            pltpu.VMEM((n, 2, 128), f32),
            pltpu.VMEM((n, 2, 128), f32),
            two, two, one, one, two, two, one, one,
        ],
        compiler_params=pltpu.CompilerParams(collective_id=0, has_side_effects=True, vmem_limit_bytes=56 * 2**20),
    )(x, route.T, owner, outer_state.reshape(n, 2, 128), momentum.reshape(n, 2, 128))
    out = back.transpose(0, 3, 1, 2, 4).reshape(inner_params.shape)
    return out, newm.reshape(momentum.shape)


def solution(mesh):
    rows = P(axes, None)
    return jax.shard_map(
        on_device,
        mesh=mesh,
        in_specs=(P(axes, None, None), P(), P(), rows, rows),
        out_specs=(P(axes, None, None), rows),
        check_vma=False,
    )
```

time: 39.2 us -> 36.9 us (0.941)
  Pallas kernels: 35.8 us -> 33.6 us
    pallas_call x1, Pallas kernels: 35.8 us -> 33.6 us  [on_device(): pl.pallas_call(functools.partial(kernel, n), out_shape=(jax.ShapeDtypeStr...]
where the time goes in v4:
time: 36.9 us; the launch traced here: 36.8 us
  Pallas kernels  33.6 us (91%)
  local copies, waits for them, and re-layouts  2.56 us (7%)
  between operations  0.65 us (2%)
    pallas_call x1, Pallas kernels, on_device(): pl.pallas_call(functools.partial(kernel, n), out_shape=(jax.ShapeDtypeStr...  33.6 us
    unnamed x4, local copies, waits for them, and re-layouts  2.56 us

profile of v4, /device:TPU:1, one launch (start us, length us, event | category | flops | bytes accessed | tf_op | source)
XLA Modules:
  0.0 36.8 jit_solution(15602567225622800332)
XLA Ops:
  0.6 33.6 %shard_map.68 = (f32[2,128,2,2,128]{4,3,2,1,0:T(2,128)}, f32[128,2,128]{2,1,0:T(2,128)}) custom-call(f32[2,128,2,2,128]{4,3,2,1,0:T(2,128)} %bitcast.10, s32[2,256]{1,0:T(2,128)} %bitcast.15, s32[2,16]{1,0:T(2,128)} %owner_hbm.1, f32[128,2,128]{2,1,0:T(2,128)} %bitcast.13, f32[128,2,128]{2,1,0:T(2,128)} %bitcast.14), custom_call_target="tpu_custom_call" | custom-call | tf_op jit(solution)/shard_map/pallas_call | solution.py:133
  34.2 0.0 copy-start
  34.2 1.9 %copy.9 = f32[2,2,32768]{2,1,0:T(2,128)} copy(f32[2,2,32768]{2,1,0:T(2,128)} %bitcast.11) | data formatting | bytes 1048576
  36.1 0.0 copy-done
  36.1 0.7 %copy.10 = f32[1,32768]{1,0:T(1,128)} copy(f32[1,32768]{1,0:T(1,128)S(1)} %bitcast.12) | data formatting | bytes 262144
Async XLA Ops:
  34.2 1.9 %copy-start = (f32[128,2,128]{2,1,0:T(2,128)S(1)}, f32[128,2,128]{2,1,0:T(2,128)}, u32[]{:S(2)}) copy-start(f32[128,2,128]{2,1,0:T(2,128)} %get-tuple-element.5) | copy-start | bytes 393220

commit v5 on v4

--- a/solution.py
+++ b/solution.py
@@ -38,6 +38,14 @@
     return y * 2 + core, z * 4 + x
 
 
+def hops(s):
+    return sum(min(a, 4 - a) for a in (s & 3, (s >> 2) & 3, (s >> 4) & 3))
+
+
+def route_order(n):
+    return sorted(range(1, n), key=lambda s: (-hops(s), s * 37 % n))
+
+
 def kernel(n, x_ref, route_hbm, owner_hbm, outer_hbm, mom_hbm, back_ref, newm_ref,
            route_ref, owner_ref, outer_ref, mom_ref, load_sem,
            own_ref, got_ref, gotown_ref, res_ref, resown_ref, backown_ref,
@@ -50,32 +58,28 @@
         load.start()
     barrier = pltpu.get_barrier_semaphore()
 
-    @pl.loop(1, n, unroll=n - 1)
-    def _(s):
+    for s in route_order(n):
         pl.semaphore_signal(barrier, inc=1, device_id=peer(s, group, path), device_id_type=MESH)
 
-    for load in loads:
-        load.wait()
-    own_ref[...] = (1 - step) * outer_ref[...] - (outer_rate * momentum_decay * momentum_decay) * mom_ref[...]
     pl.semaphore_wait(barrier, n - 1)
 
     def exchange(*moves):
         for src, dst, _, recv in moves:
             pltpu.make_async_copy(src(me), dst(me), recv).start()
 
-        @pl.loop(1, n, unroll=n - 1)
-        def _(s):
-            to = peer((s * 37) & (n - 1), group, path)
+        for s in route_order(n):
+            to = peer(s, group, path)
             rank = to[0] * 16 + to[1]
             for src, dst, sent, recv in moves:
                 pltpu.make_async_remote_copy(
                     src(rank), dst(me), sent, recv, device_id=to, device_id_type=MESH).start()
 
-    for t in range(2):
-        moves = [(lambda r: x_ref.at[:, r, t], lambda r: got_ref.at[t, r], send_sem.at[t], recv_sem.at[t])]
-        if t == 0:
-            moves.append((lambda r: own_ref.at[r], lambda r: gotown_ref.at[r], sendown_sem, recvown_sem))
-        exchange(*moves)
+    exchange((lambda r: x_ref.at[:, r, 0], lambda r: got_ref.at[0, r], send_sem.at[0], recv_sem.at[0]))
+    for load in loads:
+        load.wait()
+    own_ref[...] = (1 - step) * outer_ref[...] - (outer_rate * momentum_decay * momentum_decay) * mom_ref[...]
+    exchange((lambda r: own_ref.at[r], lambda r: gotown_ref.at[r], sendown_sem, recvown_sem))
+    exchange((lambda r: x_ref.at[:, r, 1], lambda r: got_ref.at[1, r], send_sem.at[1], recv_sem.at[1]))
 
     rows = 4 * n
     route = route_ref[...].astype(f32).astype(bf16)
@@ -124,6 +128,23 @@
     pltpu.make_async_copy(lastown, lastown, sendown2_sem).wait()
 
 
+def settle(back_ref, newm_ref, out_ref, outm_ref, block_ref, row_ref, sems):
+    size = back_ref.shape[1] // 2
+    legs = [(newm_ref, row_ref, outm_ref)]
+    for i in range(4):
+        part = (i // 2, pl.ds(i % 2 * size, size))
+        legs.append((back_ref.at[part], block_ref.at[part], out_ref.at[part]))
+    loads = [pltpu.make_async_copy(a, b, sems.at[i]) for i, (a, b, _) in enumerate(legs)]
+    stores = [pltpu.make_async_copy(b, c, sems.at[i]) for i, (_, b, c) in enumerate(legs)]
+    for load in loads:
+        load.start()
+    for load, store in zip(loads, stores):
+        load.wait()
+        store.start()
+    for store in stores:
+        store.wait()
+
+
 def on_device(inner_params, route, owner, outer_state, momentum):
     n = lax.axis_size(axes)
     x = inner_params.reshape(2, 2, n, 2, 128).transpose(0, 2, 3, 1, 4)
@@ -134,7 +155,7 @@
         functools.partial(kernel, n),
         out_shape=(jax.ShapeDtypeStruct((2, n, 2, 2, 128), f32), jax.ShapeDtypeStruct((n, 2, 128), f32)),
         in_specs=[pl.BlockSpec(memory_space=pltpu.HBM)] * 5,
-        out_specs=(vmem, vmem),
+        out_specs=(pl.BlockSpec(memory_space=pltpu.HBM), vmem),
         scratch_shapes=[
             pltpu.VMEM((2, 2 * n), jnp.int32),
             pltpu.VMEM(owner.shape, jnp.int32),
@@ -151,6 +172,15 @@
         ],
         compiler_params=pltpu.CompilerParams(collective_id=0, has_side_effects=True, vmem_limit_bytes=56 * 2**20),
     )(x, route.T, owner, outer_state.reshape(n, 2, 128), momentum.reshape(n, 2, 128))
+    hbm = pl.BlockSpec(memory_space=pltpu.HBM)
+    back, newm = pl.pallas_call(
+        settle,
+        out_shape=(jax.ShapeDtypeStruct(back.shape, f32), jax.ShapeDtypeStruct(newm.shape, f32)),
+        in_specs=[hbm, hbm],
+        out_specs=(hbm, hbm),
+        scratch_shapes=[pltpu.VMEM(back.shape, f32), pltpu.VMEM(newm.shape, f32), pltpu.SemaphoreType.DMA((5,))],
+        compiler_params=pltpu.CompilerParams(vmem_limit_bytes=56 * 2**20),
+    )(back, newm)
     out = back.transpose(0, 3, 1, 2, 4).reshape(inner_params.shape)
     return out, newm.reshape(momentum.shape)
 

time: 36.9 us -> 34.3 us (0.930)
  local copies, waits for them, and re-layouts: 2.56 us -> 0 us
    unnamed x4 -> x0, local copies, waits for them, and re-layouts: 2.56 us -> none
    pallas_call x1, Pallas kernels: 33.6 us -> 31.7 us  [on_device(): pl.pallas_call(functools.partial(kernel, n), out_shape=(jax.ShapeDtypeStr...]
    pallas_call x0 -> x1, Pallas kernels: none -> 1.86 us  [on_device(): pl.pallas_call(settle, out_shape=(jax.ShapeDtypeStruct(back.shape, f32),...]
where the time goes in v5:
time: 34.3 us; the launch traced here: 34.2 us
  Pallas kernels  33.5 us (98%)
  between operations  0.64 us (2%)
    pallas_call x1, Pallas kernels, on_device(): pl.pallas_call(functools.partial(kernel, n), out_shape=(jax.ShapeDtypeStr...  31.7 us
    pallas_call x1, Pallas kernels, on_device(): pl.pallas_call(settle, out_shape=(jax.ShapeDtypeStruct(back.shape, f32),...  1.86 us

profile of v5, /device:TPU:1, one launch (start us, length us, event | category | flops | bytes accessed | tf_op | source)
XLA Modules:
  0.0 34.2 jit_solution(1875751319001091126)
XLA Ops:
  0.6 31.7 %shard_map.68 = (f32[2,128,2,2,128]{4,3,2,1,0:T(2,128)}, f32[128,2,128]{2,1,0:T(2,128)}) custom-call(f32[2,128,2,2,128]{4,3,2,1,0:T(2,128)} %bitcast.10, s32[2,256]{1,0:T(2,128)} %bitcast.13, s32[2,16]{1,0:T(2,128)} %owner_hbm.1, f32[128,2,128]{2,1,0:T(2,128)} %bitcast.11, f32[128,2,128]{2,1,0:T(2,128)} %bitcast.12), custom_call_target="tpu_custom_call" | custom-call | tf_op jit(solution)/shard_map/pallas_call | solution.py:154
  32.3 1.9 %shard_map.69 = (f32[2,128,2,2,128]{4,3,2,1,0:T(2,128)}, f32[128,2,128]{2,1,0:T(2,128)}) custom-call(f32[2,128,2,2,128]{4,3,2,1,0:T(2,128)} %get-tuple-element.6.back_ref, f32[128,2,128]{2,1,0:T(2,128)} %get-tuple-element.7.newm_ref), custom_call_target="tpu_custom_call" | custom-call | tf_op jit(solution)/shard_map/pallas_call | solution.py:176

commit v6 on v5

--- a/solution.py
+++ b/solution.py
@@ -42,8 +42,13 @@
     return sum(min(a, 4 - a) for a in (s & 3, (s >> 2) & 3, (s >> 4) & 3))
 
 
-def route_order(n):
-    return sorted(range(1, n), key=lambda s: (-hops(s), s * 37 % n))
+def late_order():
+    pairs = [(s, zz) for s in range(128) if not s & 12 for zz in range(4)]
+    return sorted(pairs, key=lambda q: (-hops(q[0]) + q[1], q[0] * 37 % 128))
+
+
+def route_order(n, whole=False):
+    return sorted(range(0 if whole else 1, n), key=lambda s: (-hops(s), s * 37 % n))
 
 
 def kernel(n, x_ref, route_hbm, owner_hbm, outer_hbm, mom_hbm, back_ref, newm_ref,
@@ -63,22 +68,45 @@
 
     pl.semaphore_wait(barrier, n - 1)
 
-    def exchange(*moves):
-        for src, dst, _, recv in moves:
+    def exchange(*moves, late=False, cores=(0, 1), keep=True):
+        for src, dst, _, recv in moves if keep else ():
             pltpu.make_async_copy(src(me), dst(me), recv).start()
 
-        for s in route_order(n):
-            to = peer(s, group, path)
+        def post(to):
             rank = to[0] * 16 + to[1]
             for src, dst, sent, recv in moves:
                 pltpu.make_async_remote_copy(
                     src(rank), dst(me), sent, recv, device_id=to, device_id_type=MESH).start()
 
-    exchange((lambda r: x_ref.at[:, r, 0], lambda r: got_ref.at[0, r], send_sem.at[0], recv_sem.at[0]))
+        if late:
+            z = path >> 2
+            for d, zz in late_order():
+                to = peer(d, group, path)
+                to = (to[0], zz * 4 + (to[1] & 3))
+                if d:
+                    post(to)
+                else:
+                    pl.when(zz != z)(functools.partial(post, to))
+        else:
+            core = group & 1
+            for cc in cores:
+                for d in route_order(n // 2, True):
+                    to = peer(d, group, path)
+                    to = ((to[0] & 6) + cc, to[1])
+                    if d:
+                        post(to)
+                    else:
+                        pl.when(cc != core)(functools.partial(post, to))
+
+    first = (lambda r: x_ref.at[:, r, 0], lambda r: got_ref.at[0, r], send_sem.at[0], recv_sem.at[0])
+    own = (lambda r: own_ref.at[r], lambda r: gotown_ref.at[r], sendown_sem, recvown_sem)
+    exchange(first, cores=(0,))
     for load in loads:
         load.wait()
     own_ref[...] = (1 - step) * outer_ref[...] - (outer_rate * momentum_decay * momentum_decay) * mom_ref[...]
-    exchange((lambda r: own_ref.at[r], lambda r: gotown_ref.at[r], sendown_sem, recvown_sem))
+    exchange(own, cores=(0,))
+    exchange(first, cores=(1,), keep=False)
+    exchange(own, cores=(1,), keep=False)
     exchange((lambda r: x_ref.at[:, r, 1], lambda r: got_ref.at[1, r], send_sem.at[1], recv_sem.at[1]))
 
     rows = 4 * n
@@ -113,7 +141,7 @@
         moves = [(lambda r: res_ref.at[t, r], lambda r: back_ref.at[:, r, t], send2_sem.at[t], recv2_sem.at[t])]
         if t == 1:
             moves.append((lambda r: resown_ref.at[r], lambda r: backown_ref.at[r], sendown2_sem, recvown2_sem))
-        exchange(*moves)
+        exchange(*moves, late=True)
     pltpu.make_async_copy(backown_ref, backown_ref, recvown2_sem).wait()
     delta = outer_ref[...] - backown_ref[...]
     newm_ref[...] = jnp.where(owned, momentum_decay * mom_ref[...] + delta, mom_ref[...])

time: 34.3 us -> 33.1 us (0.965)
  Pallas kernels: 33.5 us -> 32.3 us
    pallas_call x1, Pallas kernels: 31.7 us -> 30.5 us  [on_device(): pl.pallas_call(functools.partial(kernel, n), out_shape=(jax.ShapeDtypeStr...]
where the time goes in v6:
time: 33.1 us; the launch traced here: 33 us
  Pallas kernels  32.3 us (98%)
  between operations  0.64 us (2%)
    pallas_call x1, Pallas kernels, on_device(): pl.pallas_call(functools.partial(kernel, n), out_shape=(jax.ShapeDtypeStr...  30.5 us
    pallas_call x1, Pallas kernels, on_device(): pl.pallas_call(settle, out_shape=(jax.ShapeDtypeStruct(back.shape, f32),...  1.86 us

profile of v6, /device:TPU:1, one launch (start us, length us, event | category | flops | bytes accessed | tf_op | source)
XLA Modules:
  0.0 33.0 jit_solution(501748828859187472)
XLA Ops:
  0.6 30.5 %shard_map.68 = (f32[2,128,2,2,128]{4,3,2,1,0:T(2,128)}, f32[128,2,128]{2,1,0:T(2,128)}) custom-call(f32[2,128,2,2,128]{4,3,2,1,0:T(2,128)} %bitcast.10, s32[2,256]{1,0:T(2,128)} %bitcast.13, s32[2,16]{1,0:T(2,128)} %owner_hbm.1, f32[128,2,128]{2,1,0:T(2,128)} %bitcast.11, f32[128,2,128]{2,1,0:T(2,128)} %bitcast.12), custom_call_target="tpu_custom_call" | custom-call | tf_op jit(solution)/shard_map/pallas_call | solution.py:182
  31.1 1.9 %shard_map.69 = (f32[2,128,2,2,128]{4,3,2,1,0:T(2,128)}, f32[128,2,128]{2,1,0:T(2,128)}) custom-call(f32[2,128,2,2,128]{4,3,2,1,0:T(2,128)} %get-tuple-element.6.back_ref, f32[128,2,128]{2,1,0:T(2,128)} %get-tuple-element.7.newm_ref), custom_call_target="tpu_custom_call" | custom-call | tf_op jit(solution)/shard_map/pallas_call | solution.py:204

commit v7 on v6

--- a/solution.py
+++ b/solution.py
@@ -43,8 +43,8 @@
 
 
 def late_order():
-    pairs = [(s, zz) for s in range(128) if not s & 12 for zz in range(4)]
-    return sorted(pairs, key=lambda q: (-hops(q[0]) + q[1], q[0] * 37 % 128))
+    spots = [(d, y, z) for d in (0, 1, 2, 3, 64, 65, 66, 67) for y in range(4) for z in range(4)]
+    return sorted(spots, key=lambda q: ((0, 1, 2, 1)[q[1]] + (0, 2, 3, 2)[q[2]] - hops(q[0]), (q[0] * 37 + q[1] * 13 + q[2] * 7) % 31))
 
 
 def route_order(n, whole=False):
@@ -68,7 +68,7 @@
 
     pl.semaphore_wait(barrier, n - 1)
 
-    def exchange(*moves, late=False, cores=(0, 1), keep=True):
+    def exchange(*moves, late=False, cores=(1, 0), keep=True):
         for src, dst, _, recv in moves if keep else ():
             pltpu.make_async_copy(src(me), dst(me), recv).start()
 
@@ -79,14 +79,14 @@
                     src(rank), dst(me), sent, recv, device_id=to, device_id_type=MESH).start()
 
         if late:
-            z = path >> 2
-            for d, zz in late_order():
+            for d, y, z in late_order():
                 to = peer(d, group, path)
-                to = (to[0], zz * 4 + (to[1] & 3))
+                to = (y * 2 + (to[0] & 1), z * 4 + (to[1] & 3))
                 if d:
                     post(to)
                 else:
-                    pl.when(zz != z)(functools.partial(post, to))
+                    away = jnp.logical_or(y != group >> 1, z != path >> 2)
+                    pl.when(away)(functools.partial(post, to))
         else:
             core = group & 1
             for cc in cores:
@@ -99,15 +99,17 @@
                         pl.when(cc != core)(functools.partial(post, to))
 
     first = (lambda r: x_ref.at[:, r, 0], lambda r: got_ref.at[0, r], send_sem.at[0], recv_sem.at[0])
-    own = (lambda r: own_ref.at[r], lambda r: gotown_ref.at[r], sendown_sem, recvown_sem)
-    exchange(first, cores=(0,))
+    own = (lambda r: own_ref.at[0, r], lambda r: gotown_ref.at[0, r], sendown_sem.at[0], recvown_sem.at[0])
+    own1 = (lambda r: own_ref.at[1, r], lambda r: gotown_ref.at[1, r], sendown_sem.at[1], recvown_sem.at[1])
+    exchange(first, cores=(1,))
     for load in loads:
         load.wait()
-    own_ref[...] = (1 - step) * outer_ref[...] - (outer_rate * momentum_decay * momentum_decay) * mom_ref[...]
-    exchange(own, cores=(0,))
-    exchange(first, cores=(1,), keep=False)
-    exchange(own, cores=(1,), keep=False)
-    exchange((lambda r: x_ref.at[:, r, 1], lambda r: got_ref.at[1, r], send_sem.at[1], recv_sem.at[1]))
+    for t in range(2):
+        own_row = (1 - step) * outer_ref[:, t, :] - (outer_rate * momentum_decay * momentum_decay) * mom_ref[:, t, :]
+        own_ref[t] = own_row.reshape(n, 1, 128)
+    exchange(own, cores=(1,))
+    exchange(first, own, cores=(0,), keep=False)
+    exchange((lambda r: x_ref.at[:, r, 1], lambda r: got_ref.at[1, r], send_sem.at[1], recv_sem.at[1]), own1)
 
     rows = 4 * n
     route = route_ref[...].astype(f32).astype(bf16)
@@ -132,28 +134,33 @@
 
     for t in range(2):
         pltpu.make_async_copy(got_ref.at[t], got_ref.at[t], recv_sem.at[t]).wait()
-        if t == 0:
-            pltpu.make_async_copy(gotown_ref, gotown_ref, recvown_sem).wait()
+        pltpu.make_async_copy(gotown_ref.at[t], gotown_ref.at[t], recvown_sem.at[t]).wait()
         mean = pick(hot, got_ref[t].reshape(rows, 128)) / counts
-        fresh = step * mean + pick(own_hot, gotown_ref[:, t, :])
+        fresh = step * mean + pick(own_hot, gotown_ref[t].reshape(n, 128))
         res_ref[t] = spread(hot2, fresh).reshape(res_ref.shape[1:])
         resown_ref[:, t, :] = spread(own_hot2, mean)
         moves = [(lambda r: res_ref.at[t, r], lambda r: back_ref.at[:, r, t], send2_sem.at[t], recv2_sem.at[t])]
         if t == 1:
             moves.append((lambda r: resown_ref.at[r], lambda r: backown_ref.at[r], sendown2_sem, recvown2_sem))
         exchange(*moves, late=True)
+    last = got_ref.at[0, pl.ds(0, n - 1)]
+    for t in range(2):
+        pltpu.make_async_copy(last, last, send_sem.at[t]).wait()
+    for t in range(2):
+        lastown = gotown_ref.at[t, pl.ds(0, n - 1)]
+        pltpu.make_async_copy(lastown, lastown, sendown_sem.at[t]).wait()
+    lastown = backown_ref.at[pl.ds(0, n - 1)]
     pltpu.make_async_copy(backown_ref, backown_ref, recvown2_sem).wait()
     delta = outer_ref[...] - backown_ref[...]
-    newm_ref[...] = jnp.where(owned, momentum_decay * mom_ref[...] + delta, mom_ref[...])
+    mom_ref[...] = jnp.where(owned, momentum_decay * mom_ref[...] + delta, mom_ref[...])
+    store = pltpu.make_async_copy(mom_ref, newm_ref, load_sem.at[1])
+    store.start()
     for t in range(2):
         pltpu.make_async_copy(got_ref.at[t], got_ref.at[t], recv2_sem.at[t]).wait()
-    last = got_ref.at[0, pl.ds(0, n - 1)]
-    for sem in (send_sem, send2_sem):
-        for t in range(2):
-            pltpu.make_async_copy(last, last, sem.at[t]).wait()
-    lastown = gotown_ref.at[pl.ds(0, n - 1)]
-    pltpu.make_async_copy(lastown, lastown, sendown_sem).wait()
+    for t in range(2):
+        pltpu.make_async_copy(last, last, send2_sem.at[t]).wait()
     pltpu.make_async_copy(lastown, lastown, sendown2_sem).wait()
+    store.wait()
 
 
 def settle(back_ref, newm_ref, out_ref, outm_ref, block_ref, row_ref, sems):
@@ -183,20 +190,20 @@
         functools.partial(kernel, n),
         out_shape=(jax.ShapeDtypeStruct((2, n, 2, 2, 128), f32), jax.ShapeDtypeStruct((n, 2, 128), f32)),
         in_specs=[pl.BlockSpec(memory_space=pltpu.HBM)] * 5,
-        out_specs=(pl.BlockSpec(memory_space=pltpu.HBM), vmem),
+        out_specs=(pl.BlockSpec(memory_space=pltpu.HBM), pl.BlockSpec(memory_space=pltpu.HBM)),
         scratch_shapes=[
             pltpu.VMEM((2, 2 * n), jnp.int32),
             pltpu.VMEM(owner.shape, jnp.int32),
             pltpu.VMEM((n, 2, 128), f32),
             pltpu.VMEM((n, 2, 128), f32),
             pltpu.SemaphoreType.DMA((4,)),
-            pltpu.VMEM((n, 2, 128), f32),
+            pltpu.VMEM((2, n, 1, 128), f32),
             pltpu.VMEM((2, n, 2, 2, 128), f32),
-            pltpu.VMEM((n, 2, 128), f32),
+            pltpu.VMEM((2, n, 1, 128), f32),
             pltpu.VMEM((2, n, 2, 2, 128), f32),
             pltpu.VMEM((n, 2, 128), f32),
             pltpu.VMEM((n, 2, 128), f32),
-            two, two, one, one, two, two, one, one,
+            two, two, two, two, two, two, one, one,
         ],
         compiler_params=pltpu.CompilerParams(collective_id=0, has_side_effects=True, vmem_limit_bytes=56 * 2**20),
     )(x, route.T, owner, outer_state.reshape(n, 2, 128), momentum.reshape(n, 2, 128))

time: 33.1 us -> 32.1 us (0.970)
  Pallas kernels: 32.3 us -> 31.3 us
    pallas_call x1, Pallas kernels: 30.5 us -> 29.5 us  [on_device(): pl.pallas_call(functools.partial(kernel, n), out_shape=(jax.ShapeDtypeStr...]
where the time goes in v7:
time: 32.1 us; the launch traced here: 32 us
  Pallas kernels  31.3 us (98%)
  between operations  0.64 us (2%)
    pallas_call x1, Pallas kernels, on_device(): pl.pallas_call(functools.partial(kernel, n), out_shape=(jax.ShapeDtypeStr...  29.5 us
    pallas_call x1, Pallas kernels, on_device(): pl.pallas_call(settle, out_shape=(jax.ShapeDtypeStruct(back.shape, f32),...  1.86 us

profile of v7, /device:TPU:1, one launch (start us, length us, event | category | flops | bytes accessed | tf_op | source)
XLA Modules:
  0.0 32.0 jit_solution(3688702676286799892)
XLA Ops:
  0.6 29.5 %shard_map.68 = (f32[2,128,2,2,128]{4,3,2,1,0:T(2,128)}, f32[128,2,128]{2,1,0:T(2,128)}) custom-call(f32[2,128,2,2,128]{4,3,2,1,0:T(2,128)} %bitcast.10, s32[2,256]{1,0:T(2,128)} %bitcast.13, s32[2,16]{1,0:T(2,128)} %owner_hbm.1, f32[128,2,128]{2,1,0:T(2,128)} %bitcast.11, f32[128,2,128]{2,1,0:T(2,128)} %bitcast.12), custom_call_target="tpu_custom_call" | custom-call | tf_op jit(solution)/shard_map/pallas_call | solution.py:189
  30.1 1.9 %shard_map.69 = (f32[2,128,2,2,128]{4,3,2,1,0:T(2,128)}, f32[128,2,128]{2,1,0:T(2,128)}) custom-call(f32[2,128,2,2,128]{4,3,2,1,0:T(2,128)} %get-tuple-element.6.back_ref, f32[128,2,128]{2,1,0:T(2,128)} %get-tuple-element.7.newm_ref), custom_call_target="tpu_custom_call" | custom-call | tf_op jit(solution)/shard_map/pallas_call | solution.py:211

commit v8 on v7

--- a/solution.py
+++ b/solution.py
@@ -44,7 +44,7 @@
 
 def late_order():
     spots = [(d, y, z) for d in (0, 1, 2, 3, 64, 65, 66, 67) for y in range(4) for z in range(4)]
-    return sorted(spots, key=lambda q: ((0, 1, 2, 1)[q[1]] + (0, 2, 3, 2)[q[2]] - hops(q[0]), (q[0] * 37 + q[1] * 13 + q[2] * 7) % 31))
+    return sorted(spots, key=lambda q: ((0, 1, 2, 1)[q[1]] + (0, 2, 4, 4)[q[2]] - hops(q[0]) - (q[0] > 63), (q[0] * 37 + q[1] * 13 + q[2] * 7) % 31))
 
 
 def route_order(n, whole=False):
@@ -137,29 +137,31 @@
         pltpu.make_async_copy(gotown_ref.at[t], gotown_ref.at[t], recvown_sem.at[t]).wait()
         mean = pick(hot, got_ref[t].reshape(rows, 128)) / counts
         fresh = step * mean + pick(own_hot, gotown_ref[t].reshape(n, 128))
+        resown_ref[t] = spread(own_hot2, mean).reshape(resown_ref.shape[1:])
         res_ref[t] = spread(hot2, fresh).reshape(res_ref.shape[1:])
-        resown_ref[:, t, :] = spread(own_hot2, mean)
-        moves = [(lambda r: res_ref.at[t, r], lambda r: back_ref.at[:, r, t], send2_sem.at[t], recv2_sem.at[t])]
-        if t == 1:
-            moves.append((lambda r: resown_ref.at[r], lambda r: backown_ref.at[r], sendown2_sem, recvown2_sem))
-        exchange(*moves, late=True)
+        exchange((lambda r: res_ref.at[t, r], lambda r: back_ref.at[:, r, t], send2_sem.at[t], recv2_sem.at[t]),
+                 (lambda r: resown_ref.at[t, r], lambda r: backown_ref.at[t, r], sendown2_sem.at[t], recvown2_sem.at[t]),
+                 late=True)
     last = got_ref.at[0, pl.ds(0, n - 1)]
     for t in range(2):
         pltpu.make_async_copy(last, last, send_sem.at[t]).wait()
     for t in range(2):
         lastown = gotown_ref.at[t, pl.ds(0, n - 1)]
         pltpu.make_async_copy(lastown, lastown, sendown_sem.at[t]).wait()
-    lastown = backown_ref.at[pl.ds(0, n - 1)]
-    pltpu.make_async_copy(backown_ref, backown_ref, recvown2_sem).wait()
-    delta = outer_ref[...] - backown_ref[...]
-    mom_ref[...] = jnp.where(owned, momentum_decay * mom_ref[...] + delta, mom_ref[...])
+    for t in range(2):
+        pltpu.make_async_copy(backown_ref.at[t], backown_ref.at[t], recvown2_sem.at[t]).wait()
+        held = mom_ref[:, t, :]
+        delta = outer_ref[:, t, :] - backown_ref[t].reshape(n, 128)
+        mom_ref[:, t, :] = jnp.where(owned, momentum_decay * held + delta, held)
     store = pltpu.make_async_copy(mom_ref, newm_ref, load_sem.at[1])
     store.start()
     for t in range(2):
         pltpu.make_async_copy(got_ref.at[t], got_ref.at[t], recv2_sem.at[t]).wait()
     for t in range(2):
         pltpu.make_async_copy(last, last, send2_sem.at[t]).wait()
-    pltpu.make_async_copy(lastown, lastown, sendown2_sem).wait()
+    for t in range(2):
+        lastown = backown_ref.at[t, pl.ds(0, n - 1)]
+        pltpu.make_async_copy(lastown, lastown, sendown2_sem.at[t]).wait()
     store.wait()
 
 
@@ -201,9 +203,9 @@
             pltpu.VMEM((2, n, 2, 2, 128), f32),
             pltpu.VMEM((2, n, 1, 128), f32),
             pltpu.VMEM((2, n, 2, 2, 128), f32),
-            pltpu.VMEM((n, 2, 128), f32),
-            pltpu.VMEM((n, 2, 128), f32),
-            two, two, two, two, two, two, one, one,
+            pltpu.VMEM((2, n, 1, 128), f32),
+            pltpu.VMEM((2, n, 1, 128), f32),
+            two, two, two, two, two, two, two, two,
         ],
         compiler_params=pltpu.CompilerParams(collective_id=0, has_side_effects=True, vmem_limit_bytes=56 * 2**20),
     )(x, route.T, owner, outer_state.reshape(n, 2, 128), momentum.reshape(n, 2, 128))

time: 32.1 us -> 32.1 us (level)
  no operation moved by 1% of the time
where the time goes in v8:
time: 32.1 us; the launch traced here: 31.9 us
  Pallas kernels  31.3 us (98%)
  between operations  0.64 us (2%)
    pallas_call x1, Pallas kernels, on_device(): pl.pallas_call(functools.partial(kernel, n), out_shape=(jax.ShapeDtypeStr...  29.4 us
    pallas_call x1, Pallas kernels, on_device(): pl.pallas_call(settle, out_shape=(jax.ShapeDtypeStruct(back.shape, f32),...  1.86 us

profile of v8, /device:TPU:1, one launch (start us, length us, event | category | flops | bytes accessed | tf_op | source)
XLA Modules:
  0.0 31.9 jit_solution(7320444565917094985)
XLA Ops:
  0.6 29.4 %shard_map.68 = (f32[2,128,2,2,128]{4,3,2,1,0:T(2,128)}, f32[128,2,128]{2,1,0:T(2,128)}) custom-call(f32[2,128,2,2,128]{4,3,2,1,0:T(2,128)} %bitcast.10, s32[2,256]{1,0:T(2,128)} %bitcast.13, s32[2,16]{1,0:T(2,128)} %owner_hbm.1, f32[128,2,128]{2,1,0:T(2,128)} %bitcast.11, f32[128,2,128]{2,1,0:T(2,128)} %bitcast.12), custom_call_target="tpu_custom_call" | custom-call | tf_op jit(solution)/shard_map/pallas_call | solution.py:191
  30.1 1.9 %shard_map.69 = (f32[2,128,2,2,128]{4,3,2,1,0:T(2,128)}, f32[128,2,128]{2,1,0:T(2,128)}) custom-call(f32[2,128,2,2,128]{4,3,2,1,0:T(2,128)} %get-tuple-element.6.back_ref, f32[128,2,128]{2,1,0:T(2,128)} %get-tuple-element.7.newm_ref), custom_call_target="tpu_custom_call" | custom-call | tf_op jit(solution)/shard_map/pallas_call | solution.py:213
